TPU v7x, 128 devices: a whole 4x4x4 slice. The times are simulated.
128 devices in a mesh: clip: 16 (over y, x), row: 8 (over z, core).
Axes of the slice: x: 4, y: 4, z: 4, core: 2. Of those that a mesh axis runs over, the one named last changes fastest.
Arguments:
- patches: bfloat16 [256, 8, 15360], P(('clip', 'row')), may hold values from -6 to 6
- clip_lengths: int32 [16], replicated, may hold values from 1 to 48, 256 in all
- stem_weight: bfloat16 [48, 192], replicated, may hold values from -0.875 to 0.875
- spatial_weight: bfloat16 [3, 3, 192, 192], replicated, may hold values from -0.15625 to 0.15625
- temporal_weight: bfloat16 [3, 192, 192], replicated, may hold values from -0.25 to 0.25
Outputs:
- block_out: bfloat16 [256, 8, 61440], P(('clip', 'row'))
Inputs may be any that keep to these rules, and one draw needn't show every extreme that they name: `clip_lengths`: the 16 clip lengths sum to 256.
All inputs are finite; a program needn't handle non-finite values.
Results may differ from a plain program's by a relative error of at most 0.0055.
Values may be sent and summed in bfloat16 or wider, within the bound.
A program may use at most 64 MiB of HBM per device.

v0:
```python
import jax
import jax.numpy as jnp
from jax import lax
from jax.sharding import PartitionSpec as P

CH = 192
PATCH = 48
COLS = 320
SLAB = 8


def find_starts(clip_lengths, frame_ids):
    clip_ends = jnp.cumsum(clip_lengths)
    clip_firsts = clip_ends - clip_lengths
    inside = clip_firsts[None, :] <= frame_ids[:, None]
    return jnp.max(jnp.where(inside, clip_firsts[None, :], 0), axis=1)


def front_work(patch_frames, stem_weight, spatial_weight):
    count = patch_frames.shape[0]
    pieces = patch_frames.reshape(count, SLAB, COLS, PATCH)
    features = jnp.einsum(
        "fhwp,pc->fhwc", pieces, stem_weight, preferred_element_type=jnp.float32
    ).astype(jnp.bfloat16)
    summed = lax.conv_general_dilated(
        features,
        spatial_weight,
        (1, 1),
        "SAME",
        dimension_numbers=("NHWC", "HWIO", "NHWC"),
        preferred_element_type=jnp.float32,
    )
    return (features, summed.astype(jnp.bfloat16))


def temporal_mix(current, previous, earlier, lag_room, temporal_weight):
    room = lag_room[:, None, None]
    first_tap = jnp.where(room >= 1, previous, current)
    second_tap = jnp.where(room >= 2, earlier, first_tap)
    summed = jnp.einsum(
        "fpc,cd->fpd", current, temporal_weight[0], preferred_element_type=jnp.float32
    )
    summed = summed + jnp.einsum(
        "fpc,cd->fpd", first_tap, temporal_weight[1], preferred_element_type=jnp.float32
    )
    summed = summed + jnp.einsum(
        "fpc,cd->fpd", second_tap, temporal_weight[2], preferred_element_type=jnp.float32
    )
    return jax.nn.silu(summed).astype(jnp.bfloat16)


def body(patches, clip_lengths, stem_weight, spatial_weight, temporal_weight):
    frames_dev = patches.shape[0]
    features, spatial = front_work(patches, stem_weight, spatial_weight)
    clip_count = lax.axis_size("clip")
    row_count = lax.axis_size("row")
    devices = clip_count * row_count
    pix_width = SLAB * COLS // devices
    incoming = lax.all_to_all(
        spatial.reshape(frames_dev, devices, pix_width * CH),
        ("clip", "row"),
        split_axis=1,
        concat_axis=0,
        tiled=True,
    )
    all_frames = devices * frames_dev
    by_pixel = incoming.reshape(all_frames, pix_width, CH)
    frame_ids = jnp.arange(all_frames, dtype=jnp.int32)
    lag_room = frame_ids - find_starts(clip_lengths, frame_ids)
    blank = jnp.zeros((2, pix_width, CH), jnp.bfloat16)
    previous = jnp.concatenate([blank[:1], by_pixel[:-1]], axis=0)
    earlier = jnp.concatenate([blank, by_pixel[:-2]], axis=0)
    branch = temporal_mix(by_pixel, previous, earlier, lag_room, temporal_weight)
    returned = lax.all_to_all(
        branch.reshape(all_frames, 1, pix_width * CH),
        ("clip", "row"),
        split_axis=0,
        concat_axis=1,
        tiled=True,
    )
    branch = returned.reshape(frames_dev, SLAB, COLS, CH)
    branch = lax.optimization_barrier(branch)
    result = (features.astype(jnp.float32) + branch.astype(jnp.float32)).astype(jnp.bfloat16)
    return result.reshape(frames_dev, SLAB, COLS * CH)


def solution(mesh):
    return jax.shard_map(
        body,
        mesh=mesh,
        in_specs=(P(("clip", "row"), None, None), P(), P(), P(), P()),
        out_specs=P(("clip", "row"), None, None),
        check_vma=False,
    )
```

profile of v0, /device:TPU:24, one launch (start us, length us, event | category | flops | bytes accessed | tf_op | source)
XLA Modules:
  0.0 184.7 jit_solution(18125919073198730199)
XLA Ops:
  0.0 0.0 copy-start
  0.0 3.5 %reshape.62 = bf16[2,8,320,48]{3,2,1,0:T(8,128)(2,1)} reshape(bf16[2,8,15360]{2,1,0:T(8,128)(2,1)} %param.5) | data formatting | bytes 983040 | tf_op jit(solution)/shard_map/reshape | solution.py:21
  3.5 2.1 %convolution_convert_fusion = bf16[2,8,320,192]{2,3,1,0:T(8,128)(2,1)S(1)} fusion(bf16[2,8,320,48]{3,2,1,0:T(8,128)(2,1)} %reshape.62, bf16[48,192]{1,0:T(8,128)(2,1)} %param.7), kind=kOutput, calls=%fused_computation.18 | convolution fusion | flops 95354880 | bytes 2476032 | tf_op jit(solution)/shard_map/fhwp,pc->fhwc/dot_general | solution.py:22
  5.6 0.0 copy-start.2
  5.6 3.4 %copy.70 = bf16[8,2,320,192]{3,0,2,1:T(8,128)(2,1)} copy(bf16[8,2,320,192]{2,3,0,1:T(8,128)(2,1)S(1)} %bitcast.50) | data formatting | bytes 3932160
  9.0 2.2 %pad.2.clone = bf16[8,2,328,192]{3,0,2,1:T(8,128)(2,1)S(1)} pad(bf16[8,2,320,192]{3,0,2,1:T(8,128)(2,1)} %copy.70, bf16[]{:T(256)} %constant.4.clone.1), padding=0_0x0_0x1_7x0_0 | pad | bytes 3981314 | tf_op jit(solution)/shard_map/convert_element_type | solution.py:24
  11.2 0.0 copy-done.2
  11.2 0.0 copy-start.6
  11.2 0.5 fusion.1
  11.7 0.0 copy-done
  11.7 0.2 copy-done.6
  11.9 6.1 %select_convert_fusion = bf16[8,16,41,192]{3,1,2,0:T(8,128)(2,1)S(1)} fusion(pred[16,41]{0,1:T(8,128)(4,1)S(1)} %copy-done.6, bf16[3,3,192,192]{3,2,1,0:T(8,128)(2,1)S(1)} %copy-done, bf16[8,2,8,43,192]{4,0,3,2,1:T(8,128)(2,1)S(1)} %fusion.1), kind=kOutput, calls=%fused_computation.2 | convolution fusion | flops 3194142720 | bytes 4792976 | tf_op jit(solution)/shard_map/conv_general_dilated | solution.py:25
  18.1 0.9 copy.50
  19.0 0.2 slice_bitcast_fusion
  19.2 0.6 copy.51
  19.7 3.6 %reshape.63 = bf16[2,128,3840]{2,1,0:T(8,128)(2,1)} reshape(bf16[2,8,320,192]{3,2,1,0:T(8,128)(2,1)S(1)} %copy.51) | data formatting | bytes 3932160 | tf_op jit(solution)/shard_map/reshape | solution.py:60
  23.3 4.9 %copy.52 = bf16[2,128,3840]{2,0,1:T(2,128)(2,1)} copy(bf16[2,128,3840]{2,1,0:T(8,128)(2,1)} %reshape.63) | data formatting | bytes 3932160 | tf_op jit(solution)/shard_map/reshape | solution.py:60
  28.2 10.7 %all-to-all-start = ((bf16[2,128,3840]{2,0,1:T(2,128)(2,1)}), bf16[2,128,3840]{2,0,1:T(2,128)(2,1)}, u32[]{:S(2)}, u32[]{:S(2)}) async-start(bf16[2,128,3840]{2,0,1:T(2,128)(2,1)} %copy.52), calls=%async_computation | async-start | bytes 3932160 | tf_op jit(solution)/shard_map/all_to_all | solution.py:59
  38.9 0.0 copy-done.5
  38.9 0.1 copy.55
  39.0 0.1 reduce
  39.1 0.1 select_reduce_fusion
  39.2 27.3 %all-to-all-done = bf16[2,128,3840]{2,0,1:T(2,128)(2,1)} async-done(((bf16[2,128,3840]{2,0,1:T(2,128)(2,1)}), bf16[2,128,3840]{2,0,1:T(2,128)(2,1)}, u32[]{:S(2)}, u32[]{:S(2)}) %all-to-all-start) | async-done | bytes 1966112 | tf_op jit(solution)/shard_map/all_to_all | solution.py:59
  66.5 6.0 %reshape.64 = bf16[256,20,192]{2,1,0:T(8,128)(2,1)S(1)} reshape(bf16[128,2,1,3840]{3,1,0,2:T(2,128)(2,1)} %bitcast.8) | data formatting | bytes 3932160 | tf_op jit(solution)/shard_map/reshape | solution.py:67
  72.5 4.1 %slice.30 = bf16[127,2,1,3840]{3,1,0,2:T(2,128)(2,1)} slice(bf16[128,2,1,3840]{3,1,0,2:T(2,128)(2,1)} %bitcast.8), slice={[0:127], [0:2], [0:1], [0:3840]} | slice | bytes 3901440 | tf_op jit(solution)/shard_map/slice | solution.py:72
  76.6 1.9 %slice.29 = bf16[255,20,192]{2,1,0:T(8,128)(2,1)} slice(bf16[256,20,192]{2,1,0:T(8,128)(2,1)S(1)} %reshape.64), slice={[0:255], [0:20], [0:192]} | slice | bytes 3916800 | tf_op jit(solution)/shard_map/slice | solution.py:71
  78.5 7.2 %slice.23 = bf16[254,20,192]{2,1,0:T(8,128)(2,1)} reshape(bf16[127,2,1,3840]{3,1,0,2:T(2,128)(2,1)} %slice.30) | data formatting | bytes 3901440 | tf_op jit(solution)/shard_map/slice | solution.py:72
  85.7 4.4 %pad_select_fusion = (bf16[256,20,192]{2,1,0:T(8,128)(2,1)S(1)}, bf16[256,20,192]{2,1,0:T(8,128)(2,1)S(1)}) fusion(bf16[254,20,192]{2,1,0:T(8,128)(2,1)} %slice.23, pred[256]{0:T(512)(128)(4,1)S(1)} %get-tuple-element.8, bf16[256,20,192]{2,1,0:T(8,128)(2,1)S(1)} %reshape.64, bf16[255,20,192]{2,1,0:T(8,128)(2,1)} %slice.29, pred[256]{0:T(512)(128)(4,1)S(1)} %get-tuple-element.7), kind=kLoop, calls=%fused_computation.5 | loop fusion | flops 1966080 | bytes 9807872 | tf_op jit(solution)/shard_map/jit(_where)/select_n | solution.py:39
  90.2 0.0 copy-done.4
  90.2 1.1 fusion.5
  91.2 1.1 fusion.7
  92.3 3.1 %multiply_convert_fusion = bf16[256,20,192]{0,2,1:T(8,128)(2,1)} fusion(f32[256,20,192]{0,2,1:T(8,128)S(1)} %fusion.5, f32[256,20,192]{0,2,1:T(8,128)S(1)} %fusion.7, bf16[256,20,192]{2,1,0:T(8,128)(2,1)S(1)} %reshape.64, bf16[3,192,192]{2,1,0:T(8,128)(2,1)S(1)} %copy-done.4), kind=kOutput, calls=%fused_computation.4 | convolution fusion | flops 384368640 | bytes 13074432 | tf_op jit(solution)/shard_map/fpc,cd->fpd/dot_general | solution.py:40
  95.4 0.5 broadcast.27
  95.9 3.6 %reduce.2 = bf16[256,3840]{0,1:T(8,128)(2,1)S(1)} reduce(bf16[256,1,3840]{0,2,1:T(8,128)(2,1)} %bitcast.55, bf16[]{:T(256)} %broadcast.27), dimensions={1}, to_apply=%copy.60.reduce_sub_computation | reduce | bytes 3932162 | tf_op jit(solution)/shard_map/reshape | solution.py:75
  99.6 2.3 %copy.86 = bf16[256,3840]{1,0:T(8,128)(2,1)} copy(bf16[256,3840]{0,1:T(8,128)(2,1)S(1)} %reduce.2) | data formatting | bytes 3932160
  101.8 4.1 %reshape.86 = bf16[128,2,3840]{2,1,0:T(2,128)(2,1)S(1)} reshape(bf16[256,3840]{1,0:T(8,128)(2,1)} %copy.86) | data formatting | bytes 3932160
  105.9 33.7 %all_to_all.30 = bf16[128,2,3840]{2,1,0:T(2,128)(2,1)} all-to-all(bf16[128,2,3840]{2,1,0:T(2,128)(2,1)S(1)} %reshape.86), channel_id=1, replica_groups=mesh['clip'=16,'row'=8] {'clip','row'}, dimensions={0} | all-to-all | bytes 3932160 | tf_op jit(solution)/shard_map/all_to_all | solution.py:74
  139.6 10.2 %reshape.87 = bf16[256,1,3840]{2,1,0:T(2,128)(2,1)} reshape(bf16[128,2,3840]{2,1,0:T(2,128)(2,1)} %all_to_all.30) | data formatting | bytes 3932160
  149.8 12.0 %reduce.1 = bf16[256,3840]{1,0:T(8,128)(2,1)S(1)} reduce(bf16[256,1,3840]{2,1,0:T(2,128)(2,1)} %reshape.87, bf16[]{:T(256)} %constant.28), dimensions={1}, to_apply=%all_to_all.25.reduce_sub_computation | reduce | bytes 3932162 | tf_op jit(solution)/shard_map/all_to_all | solution.py:74
  161.9 1.7 all_to_all.26
  163.6 1.7 copy.61
  165.3 4.1 %reshape.68 = bf16[2,8,320,192]{3,2,1,0:T(8,128)(2,1)} reshape(bf16[2,128,1,3840]{3,1,0,2:T(8,128)(2,1)S(1)} %copy.61) | data formatting | bytes 3932160 | tf_op jit(solution)/shard_map/reshape | solution.py:81
  169.5 4.6 %copy.62 = bf16[2,8,320,192]{2,3,1,0:T(8,128)(2,1)} copy(bf16[2,8,320,192]{3,2,1,0:T(8,128)(2,1)} %reshape.68) | data formatting | bytes 3932160 | tf_op jit(solution)/shard_map/optimization_barrier | solution.py:82
  174.0 0.0 copy-done.3
  174.0 3.7 %add_convert_fusion = bf16[2,8,320,192]{2,3,1,0:T(8,128)(2,1)} fusion(bf16[2,8,320,192]{2,3,1,0:T(8,128)(2,1)} %copy.62, bf16[2,8,320,192]{2,3,1,0:T(8,128)(2,1)S(1)} %copy-done.3), kind=kLoop, calls=%fused_computation.3 | loop fusion | flops 3932160 | bytes 5898240 | tf_op jit(solution)/shard_map/convert_element_type | solution.py:83
  177.8 3.1 %copy.63 = bf16[2,8,320,192]{3,2,1,0:T(8,128)(2,1)S(1)} copy(bf16[2,8,320,192]{2,3,1,0:T(8,128)(2,1)} %add_convert_fusion) | data formatting | bytes 3932160 | tf_op jit(solution)/shard_map/convert_element_type | solution.py:83
  180.9 3.8 %reshape.69 = bf16[2,8,61440]{2,1,0:T(8,128)(2,1)} reshape(bf16[2,8,320,192]{3,2,1,0:T(8,128)(2,1)S(1)} %copy.63) | data formatting | bytes 3932160 | tf_op jit(solution)/shard_map/reshape | solution.py:84
  184.7 0.0 copy-done.1
  (8 shorter events, 0.1 us)
Async XLA Ops:
  0.0 11.7 %copy-start = (bf16[3,3,192,192]{3,2,1,0:T(8,128)(2,1)S(1)}, bf16[3,3,192,192]{3,2,1,0:T(8,128)(2,1)}, u32[]{:S(2)}) copy-start(bf16[3,3,192,192]{3,2,1,0:T(8,128)(2,1)} %param.8) | copy-start | bytes 1990660
  5.6 5.6 %copy-start.2 = (bf16[2,8,320,192]{2,3,1,0:T(8,128)(2,1)}, bf16[2,8,320,192]{2,3,1,0:T(8,128)(2,1)S(1)}, u32[]{:S(2)}) copy-start(bf16[2,8,320,192]{2,3,1,0:T(8,128)(2,1)S(1)} %convolution_convert_fusion) | copy-start | bytes 5898244
  11.2 0.7 copy-start.6
  28.2 10.7 %copy-start.5 = (s32[16]{0:T(128)S(1)}, s32[16]{0:T(128)}, u32[]{:S(2)}) copy-start(s32[16]{0:T(128)} %param.6) | copy-start | bytes 196
  28.2 38.3 %all-to-all-start = ((bf16[2,128,3840]{2,0,1:T(2,128)(2,1)}), bf16[2,128,3840]{2,0,1:T(2,128)(2,1)}, u32[]{:S(2)}, u32[]{:S(2)}) async-start(bf16[2,128,3840]{2,0,1:T(2,128)(2,1)} %copy.52), calls=%async_computation | async-start | bytes 3932160 | tf_op jit(solution)/shard_map/all_to_all | solution.py:59
  85.7 4.4 %copy-start.4 = (bf16[3,192,192]{2,1,0:T(8,128)(2,1)S(1)}, bf16[3,192,192]{2,1,0:T(8,128)(2,1)}, u32[]{:S(2)}) copy-start(bf16[3,192,192]{2,1,0:T(8,128)(2,1)} %param.9) | copy-start | bytes 663556
  169.5 4.6 %copy-start.3 = (bf16[2,8,320,192]{2,3,1,0:T(8,128)(2,1)S(1)}, bf16[2,8,320,192]{2,3,1,0:T(8,128)(2,1)}, u32[]{:S(2)}) copy-start(bf16[2,8,320,192]{2,3,1,0:T(8,128)(2,1)} %copy-done.2) | copy-start | bytes 5898244
  177.8 6.9 %copy-start.1 = (bf16[3,3,192,192]{3,2,1,0:T(8,128)(2,1)S(1)}, bf16[3,3,192,192]{3,2,1,0:T(8,128)(2,1)}, u32[]{:S(2)}) copy-start(bf16[3,3,192,192]{3,2,1,0:T(8,128)(2,1)} %param.8) | copy-start | bytes 1990660
where the time goes:
time: 188 us; the launch traced here: 185 us
  local copies, waits for them, and re-layouts  74.8 us (40%)
  blocking collectives  33.7 us (18%)
  waiting for transfers between devices  27.3 us (15%)
  other arithmetic  24.5 us (13%)
  matrix products  13.5 us (7%)
  starting transfers between devices  10.7 us (6%)
    all_to_all x1, blocking collectives, body(): lax.all_to_all(branch.reshape(all_frames, 1, pix_width * CH), ('clip', 'r...  33.7 us
    all_to_all x1, waiting for transfers between devices, body(): lax.all_to_all(spatial.reshape(frames_dev, devices, pix_width * CH), ('cl...  27.3 us
    unnamed x18, local copies, waits for them, and re-layouts  20.2 us
    all_to_all x1, other arithmetic, body(): lax.all_to_all(branch.reshape(all_frames, 1, pix_width * CH), ('clip', 'r...  12 us
    slice x2, local copies, waits for them, and re-layouts, body(): earlier = jnp.concatenate([blank, by_pixel[:-2]], axis=0)  11.4 us
    all_to_all x1, starting transfers between devices, body(): lax.all_to_all(spatial.reshape(frames_dev, devices, pix_width * CH), ('cl...  10.7 us
    reshape x2, local copies, waits for them, and re-layouts, body(): spatial.reshape(frames_dev, devices, pix_width * CH)  8.44 us
    conv_general_dilated x1, matrix products, front_work(): lax.conv_general_dilated(features, spatial_weight, (1, 1), 'SAME', dimens...  6.13 us
  transfers between devices with their start and end apart: 1, of which 1 were waited for; matrix products, arithmetic and copies ran while one was open for 0% of the time, Pallas kernels for 0%

commit v1 on v0

v1 whole, which is shorter than its diff:
```python
import jax
import jax.numpy as jnp
from jax import lax
from jax.experimental import pallas as pl
from jax.experimental.pallas import tpu as pltpu
from jax.sharding import PartitionSpec as P

MESH = pl.DeviceIdType.MESH
BF16, F32 = jnp.bfloat16, jnp.float32

CH = 192
PATCH = 48
COLS = 320
SLAB = 8
LANES = COLS * PATCH
PAIRS = 20
TILES = 6
HALF = 320
CHUNKS = 2
LAST = 127
READS = ((0, 3), (0, 1), (0, 1), (1, 2), (1, 2), (2, 4))


def lane_block(tile, block):
    if tile == 0:
        return block if block < 12 else block - 16
    if tile == 5:
        return block + 16 if block < 12 else block
    return block if tile < 3 else block + 8


def mix(a, b):
    return jnp.dot(a, b, preferred_element_type=F32)


def spread(values, keep, kind):
    rows = values.shape[0]
    wide = jnp.concatenate([values, jnp.zeros((rows, 64), F32)], axis=1)
    back = pltpu.roll(wide, 192, 1)
    ahead = pltpu.roll(wide, 64, 1)
    keep[kind + (0,)] = wide[:, :128].astype(BF16)
    keep[kind + (1,)] = back[:, :128].astype(BF16)
    keep[kind + (2,)] = wide[:, 128:].astype(BF16)
    keep[kind + (3,)] = ahead[:, :128].astype(BF16)


def block_of(small, tile, half, block, base, first, count):
    lanes = 2 * tile + half
    pixel = 2 * (lanes // 3)
    place = lane_block(tile, block)

    def take(pix, arrangement):
        row = place - 3 * (pix + first)
        if 0 <= row < count:
            return small(arrangement, base + 16 * row)
        return None

    if lanes % 3 == 0:
        parts = [take(pixel, 0)]
    elif lanes % 3 == 2:
        parts = [take(pixel + 1, 1)]
    else:
        parts = [take(pixel, 2), take(pixel + 1, 3)]
    parts = [part for part in parts if part is not None]
    if not parts:
        return jnp.zeros((16, 128), BF16)
    return parts[0] if len(parts) == 1 else parts[0] + parts[1]


def kernel(
    lengths, patches, stem_hbm, spatial_hbm, temporal_hbm, out,
    own, halo, stem, spatial, temporal, folded, small, small_stem, wide, wide_stem, rows, acc, feats,
    load_sem, send_sem, recv_sem,
):
    clip, row = lax.axis_index("clip"), lax.axis_index("row")
    me = clip * 8 + row

    def place(device):
        return (device // 8, lax.rem(device, 8))

    loads = [
        pltpu.make_async_copy(spatial_hbm, spatial, load_sem.at[0]),
        pltpu.make_async_copy(stem_hbm, stem, load_sem.at[1]),
        pltpu.make_async_copy(temporal_hbm, temporal, load_sem.at[2]),
        pltpu.make_async_copy(patches, own.at[:, :, pl.ds(128, LANES)], load_sem.at[3]),
    ]
    barrier = pltpu.get_barrier_semaphore()

    @pl.when(me > 0)
    def _():
        pl.semaphore_signal(barrier, inc=1, device_id=place(me - 1), device_id_type=MESH)

    for load in loads:
        load.start()

    cuts = [PAIRS * c // CHUNKS for c in range(CHUNKS + 1)]
    edges = [0] + [768 * cut + 128 for cut in cuts[1:-1]] + [LANES]
    sends = [
        pltpu.make_async_remote_copy(
            patches.at[:, :, pl.ds(lo, hi - lo)],
            halo.at[:, :, pl.ds(128 + lo, hi - lo)],
            send_sem.at[c],
            recv_sem.at[c],
            device_id=place(jnp.minimum(me + 1, LAST)),
            device_id_type=MESH,
        )
        for c, (lo, hi) in enumerate(zip(edges[:-1], edges[1:]))
    ]

    @pl.when(me < LAST)
    def _():
        pl.semaphore_wait(barrier, 1)
        for send in sends:
            send.start()

    first, total = jnp.int32(0), jnp.int32(0)
    first_next = jnp.int32(0)
    for k in range(16):
        first = jnp.where(total <= 2 * me, total, first)
        first_next = jnp.where(total <= 2 * me + 1, total, first_next)
        total = total + lengths[k]
    room0 = 2 * me - first
    room1 = 2 * me + 1 - first_next

    side = jnp.zeros((2, SLAB, 128), BF16)
    for ref in (own, halo):
        ref[:, :, :128] = side
        ref[:, :, LANES + 128:] = side

    loads[0].wait()
    loads[1].wait()
    for tap in range(9):
        folded[48 * tap : 48 * tap + 48] = mix(stem[...], spatial[tap // 3, tap % 3])
    spread(stem[...].astype(F32), small_stem, ())
    loads[2].wait()
    upper = folded[...].astype(BF16)
    lower = (folded[...] - upper.astype(F32)).astype(BF16)
    for t in range(3):
        spread(mix(upper, temporal[t]) + mix(lower, temporal[t]), small, (t,))

    def widen(tap, carry):
        t, a = tap // 3, lax.rem(tap, 3)
        base = a * 144
        for tile in range(TILES):
            for half in range(2):
                for block in range(16):
                    value = block_of(
                        lambda arrangement, row: small[t, arrangement, pl.ds(pl.multiple_of(row, 16), 16)],
                        tile, half, block, base, -1, 9,
                    )
                    where = pl.ds(pl.multiple_of(tap * 256 + 16 * block, 16), 16)
                    wide[tile, where, 128 * half : 128 * half + 128] = value
        return carry

    lax.fori_loop(0, 9, widen, 0)
    for tile in range(TILES):
        for half in range(2):
            for block in range(16):
                wide_stem[tile, 16 * block : 16 * block + 16, 128 * half : 128 * half + 128] = block_of(
                    lambda arrangement, row: small_stem[arrangement, row : row + 16], tile, half, block, 0, 0, 3
                )

    band = lax.broadcasted_iota(jnp.int32, (SLAB, 1024), 0)
    lane = lax.broadcasted_iota(jnp.int32, (SLAB, 128), 1)

    def put(source, t, frame, pair):
        shifted = (
            jnp.where(band == 0, 0.0, pltpu.roll(source, 1, 0)),
            source,
            jnp.where(band == SLAB - 1, 0.0, pltpu.roll(source, SLAB - 1, 0)),
        )
        where = pl.ds(pl.multiple_of(frame * HALF + pair * 16, 16), 16)
        for a, values in enumerate(shifted):
            groups = []
            for at in (0, 384):
                tiles = [values[:, at + 128 * i : at + 128 * i + 128] for i in range(5)]
                groups.append(
                    (tiles[1], tiles[2], tiles[3],
                     jnp.where(lane < 64, tiles[2], tiles[0]), jnp.where(lane < 64, tiles[4], tiles[2]))
                )
            for i in range(5):
                both = jnp.concatenate([groups[0][i], groups[1][i]], axis=0)
                rows[t, a, i, where] = both.astype(BF16)

    def lanes_of(ref, frame, pair):
        return ref[frame, :, pl.ds(pl.multiple_of(pair * 768, 128), 1024)].astype(F32)

    loads[3].wait()

    def own_rows(pair, carry):
        own0, own1 = lanes_of(own, 0, pair), lanes_of(own, 1, pair)
        put(own0, 0, 0, pair)
        put(own1, 0, 1, pair)
        put(jnp.where(room1 >= 1, own0, own1), 1, 1, pair)
        return carry

    lax.fori_loop(0, PAIRS, own_rows, 0)

    def left_side(t, tile, lo, count):
        i, j = READS[tile]
        return jnp.concatenate(
            [rows[t, a, k, lo : lo + count] for a in range(3) for k in (i, j)], axis=1
        )

    for tile in range(TILES):
        i, j = READS[tile]
        centre = jnp.concatenate([rows[0, 1, i], rows[0, 1, j]], axis=1)
        feats[tile] = mix(centre, wide_stem[tile]).astype(BF16)
        acc[tile] = mix(left_side(0, tile, 0, 2 * HALF), wide[tile, 0:768])
        acc[tile, HALF:] += mix(left_side(1, tile, HALF, HALF), wide[tile, 768:1536])

    def halo_rows(pair, carry):
        own0, own1 = lanes_of(own, 0, pair), lanes_of(own, 1, pair)
        halo0, halo1 = lanes_of(halo, 0, pair), lanes_of(halo, 1, pair)
        tap01 = jnp.where(room0 >= 1, halo1, own0)
        put(tap01, 1, 0, pair)
        put(jnp.where(room0 >= 2, halo0, tap01), 2, 0, pair)
        tap11 = jnp.where(room1 >= 1, own0, own1)
        put(jnp.where(room1 >= 2, halo1, tap11), 2, 1, pair)
        return carry

    for c in range(CHUNKS):
        @pl.when(me > 0)
        def _():
            sends[c].wait_recv()

        lax.fori_loop(cuts[c], cuts[c + 1], halo_rows, 0)
        lo, count = 16 * cuts[c], 16 * (cuts[c + 1] - cuts[c])
        for tile in range(TILES):
            tap1 = mix(left_side(1, tile, lo, count), wide[tile, 768:1536])
            for frame in range(2):
                at = frame * HALF + lo
                value = acc[tile, at : at + count] + mix(left_side(2, tile, at, count), wide[tile, 1536:])
                if frame == 0:
                    value = value + tap1
                branch = (value * (0.5 * jnp.tanh(0.5 * value) + 0.5)).astype(BF16)
                result = (feats[tile, at : at + count].astype(F32) + branch.astype(F32)).astype(BF16)
                for g in range(count // 8):
                    to = (lo // 8 + g) * 1536 + 256 * tile
                    out[frame, :, to : to + 256] = result[8 * g : 8 * g + 8]

    @pl.when(me < LAST)
    def _():
        for send in sends:
            send.wait_send()


def body(patches, clip_lengths, stem_weight, spatial_weight, temporal_weight):
    hbm = pl.BlockSpec(memory_space=pltpu.HBM)
    return pl.pallas_call(
        kernel,
        out_shape=pltpu.VMEM((2, SLAB, COLS * CH), BF16),
        in_specs=[pl.BlockSpec(memory_space=pltpu.SMEM), hbm, hbm, hbm, hbm],
        scratch_shapes=[
            pltpu.VMEM((2, SLAB, LANES + 256), BF16),
            pltpu.VMEM((2, SLAB, LANES + 256), BF16),
            pltpu.VMEM((PATCH, CH), BF16),
            pltpu.VMEM((3, 3, CH, CH), BF16),
            pltpu.VMEM((3, CH, CH), BF16),
            pltpu.VMEM((9 * PATCH, CH), F32),
            pltpu.VMEM((3, 4, 9 * PATCH, 128), BF16),
            pltpu.VMEM((4, PATCH, 128), BF16),
            pltpu.VMEM((TILES, 9 * 256, 256), BF16),
            pltpu.VMEM((TILES, 256, 256), BF16),
            pltpu.VMEM((3, 3, 5, 2 * HALF, 128), BF16),
            pltpu.VMEM((TILES, 2 * HALF, 256), F32),
            pltpu.VMEM((TILES, 2 * HALF, 256), BF16),
            pltpu.SemaphoreType.DMA((4,)),
            pltpu.SemaphoreType.DMA((CHUNKS,)),
            pltpu.SemaphoreType.DMA((CHUNKS,)),
        ],
        compiler_params=pltpu.CompilerParams(
            collective_id=0, has_side_effects=True, vmem_limit_bytes=44 << 20
        ),
        cost_estimate=pl.CostEstimate(flops=10_000_000_000, bytes_accessed=4_000_000, transcendentals=1_000_000),
    )(clip_lengths, patches, stem_weight, spatial_weight, temporal_weight)


def solution(mesh):
    return jax.shard_map(
        body,
        mesh=mesh,
        in_specs=(P(("clip", "row"), None, None), P(), P(), P(), P()),
        out_specs=P(("clip", "row"), None, None),
        check_vma=False,
    )
```

time: 188 us -> 21.4 us (0.11); the launches traced: 185 us -> 21.1 us
  local copies, waits for them, and re-layouts: 74.8 us -> 5.82 us
  blocking collectives: 33.7 us -> 0 us
  waiting for transfers between devices: 27.3 us -> 0 us
  other arithmetic: 24.5 us -> 0 us
  Pallas kernels: 0 us -> 15.3 us
  matrix products: 13.5 us -> 0 us
  starting transfers between devices: 10.7 us -> 0 us
    all_to_all x1 -> x0, blocking collectives: 33.7 us -> none  [body(): lax.all_to_all(branch.reshape(all_frames, 1, pix_width * CH), ('clip', 'r...]
    all_to_all x1 -> x0, waiting for transfers between devices: 27.3 us -> none  [body(): lax.all_to_all(spatial.reshape(frames_dev, devices, pix_width * CH), ('cl...]
    reshape x7 -> x0, local copies, waits for them, and re-layouts: 26.4 us -> none  [the longest x2 8.44 us: body(): spatial.reshape(frames_dev, devices, pix_width * CH)]
    pallas_call x0 -> x1, Pallas kernels: none -> 15.3 us  [body(): pl.pallas_call(kernel, out_shape=pltpu.VMEM((2, SLAB, COLS * CH), BF16),...]
    unnamed x18 -> x11, local copies, waits for them, and re-layouts: 20.2 us -> 5.82 us
    slice x3 -> x0, local copies, waits for them, and re-layouts: 13.2 us -> none  [the longest x2 11.4 us: body(): earlier = jnp.concatenate([blank, by_pixel[:-2]], axis=0)]
    all_to_all x1 -> x0, other arithmetic: 12 us -> none  [body(): lax.all_to_all(branch.reshape(all_frames, 1, pix_width * CH), ('clip', 'r...]
    all_to_all x1 -> x0, starting transfers between devices: 10.7 us -> none  [body(): lax.all_to_all(spatial.reshape(frames_dev, devices, pix_width * CH), ('cl...]
  transfers between devices with their start and end apart: 1 -> 0, of which waited for: 1 -> 0; matrix products, arithmetic and copies ran while one was open for 0% -> 0% of each run, Pallas kernels for 0% -> 0%
where the time goes in v1:
time: 21.4 us; the launch traced here: 21.1 us
  Pallas kernels  15.3 us (71%)
  local copies, waits for them, and re-layouts  5.82 us (27%)
    pallas_call x1, Pallas kernels, body(): pl.pallas_call(kernel, out_shape=pltpu.VMEM((2, SLAB, COLS * CH), BF16),...  15.3 us
    unnamed x11, local copies, waits for them, and re-layouts  5.82 us

profile of v1, /device:TPU:24, one launch (start us, length us, event | category | flops | bytes accessed | tf_op | source)
XLA Modules:
  0.0 21.1 jit_solution(12563305921653467904)
XLA Ops:
  0.0 0.0 copy-start
  0.0 1.2 %copy-done = bf16[3,3,192,192]{3,2,1,0:T(8,128)(2,1)S(1)} copy-done((bf16[3,3,192,192]{3,2,1,0:T(8,128)(2,1)S(1)}, bf16[3,3,192,192]{3,2,1,0:T(8,128)(2,1)}, u32[]{:S(2)}) %copy-start) | copy-done | bytes 663576
  1.2 0.0 copy-start.1
  1.2 1.0 %copy-done.1 = bf16[2,8,15360]{2,1,0:T(8,128)(2,1)S(1)} copy-done((bf16[2,8,15360]{2,1,0:T(8,128)(2,1)S(1)}, bf16[2,8,15360]{2,1,0:T(8,128)(2,1)}, u32[]{:S(2)}) %copy-start.1) | copy-done | bytes 491544
  2.2 0.0 copy-start.2
  2.2 1.0 %copy-done.2 = bf16[3,192,192]{2,1,0:T(8,128)(2,1)S(1)} copy-done((bf16[3,192,192]{2,1,0:T(8,128)(2,1)S(1)}, bf16[3,192,192]{2,1,0:T(8,128)(2,1)}, u32[]{:S(2)}) %copy-start.2) | copy-done | bytes 221208
  3.2 0.0 copy-start.3
  3.2 0.7 %copy-done.3 = bf16[48,192]{1,0:T(8,128)(2,1)S(1)} copy-done((bf16[48,192]{1,0:T(8,128)(2,1)S(1)}, bf16[48,192]{1,0:T(8,128)(2,1)}, u32[]{:S(2)}) %copy-start.3) | copy-done | bytes 18456
  3.9 0.0 copy-start.4
  3.9 0.7 %copy-done.4 = s32[16]{0:T(128)S(1)} copy-done((s32[16]{0:T(128)S(1)}, s32[16]{0:T(128)}, u32[]{:S(2)}) %copy-start.4) | copy-done | bytes 88
  4.6 15.3 %shard_map.55 = bf16[2,8,61440]{2,1,0:T(8,128)(2,1)S(1)} custom-call(s32[16]{0:T(128)S(1)} %copy-done.4, bf16[2,8,15360]{2,1,0:T(8,128)(2,1)S(1)} %copy-done.1, bf16[48,192]{1,0:T(8,128)(2,1)S(1)} %copy-done.3, bf16[3,3,192,192]{3,2,1,0:T(8,128)(2,1)S(1)} %copy-done, bf16[3,192,192]{2,1,0:T(8,128)(2,1)S(1)} %copy-done.2), custom_call_target="tpu_custom_call" | custom-call | flops 10000000000 | bytes 4000000 | tf_op jit(solution)/shard_map/pallas_call | solution.py:250
  19.8 1.3 %copy.7 = bf16[2,8,61440]{2,1,0:T(8,128)(2,1)} copy(bf16[2,8,61440]{2,1,0:T(8,128)(2,1)S(1)} %shard_map.55) | data formatting | bytes 3932160
Async XLA Ops:
  0.0 1.2 %copy-start = (bf16[3,3,192,192]{3,2,1,0:T(8,128)(2,1)S(1)}, bf16[3,3,192,192]{3,2,1,0:T(8,128)(2,1)}, u32[]{:S(2)}) copy-start(bf16[3,3,192,192]{3,2,1,0:T(8,128)(2,1)} %spatial_hbm.1) | copy-start | bytes 1990660
  1.2 1.0 %copy-start.1 = (bf16[2,8,15360]{2,1,0:T(8,128)(2,1)S(1)}, bf16[2,8,15360]{2,1,0:T(8,128)(2,1)}, u32[]{:S(2)}) copy-start(bf16[2,8,15360]{2,1,0:T(8,128)(2,1)} %patches.1) | copy-start | bytes 1474564
  2.2 1.0 %copy-start.2 = (bf16[3,192,192]{2,1,0:T(8,128)(2,1)S(1)}, bf16[3,192,192]{2,1,0:T(8,128)(2,1)}, u32[]{:S(2)}) copy-start(bf16[3,192,192]{2,1,0:T(8,128)(2,1)} %temporal_hbm.1) | copy-start | bytes 663556
  3.2 0.7 %copy-start.3 = (bf16[48,192]{1,0:T(8,128)(2,1)S(1)}, bf16[48,192]{1,0:T(8,128)(2,1)}, u32[]{:S(2)}) copy-start(bf16[48,192]{1,0:T(8,128)(2,1)} %stem_hbm.1) | copy-start | bytes 55300
  3.9 0.7 %copy-start.4 = (s32[16]{0:T(128)S(1)}, s32[16]{0:T(128)}, u32[]{:S(2)}) copy-start(s32[16]{0:T(128)} %lengths.1) | copy-start | bytes 196

commit v2 on v1

v2 whole, which is shorter than its diff:
```python
import jax
import jax.numpy as jnp
from jax import lax
from jax.experimental import pallas as pl
from jax.experimental.pallas import tpu as pltpu
from jax.sharding import PartitionSpec as P

MESH = pl.DeviceIdType.MESH
BF16, F32 = jnp.bfloat16, jnp.float32

CH = 192
PATCH = 48
COLS = 320
SLAB = 8
LANES = COLS * PATCH
GROUPS = 40
TILES = 3
HALF = 640
CUTS = (0, 10, 20, 30, 40)
CHUNKS = len(CUTS) - 1
LAST = 127
STEP = 160
READS = ((0, 2), (0, 1), (0, 1))


def lane_block(tile, block):
    return block - 16 if tile == 0 and block >= 12 else block


def mix(a, b):
    return jnp.dot(a, b, preferred_element_type=F32)


def spread(values, keep, kind):
    rows = values.shape[0]
    wide = jnp.concatenate([values, jnp.zeros((rows, 64), F32)], axis=1)
    back = pltpu.roll(wide, 192, 1)
    ahead = pltpu.roll(wide, 64, 1)
    keep[kind + (0,)] = wide[:, :128].astype(BF16)
    keep[kind + (1,)] = back[:, :128].astype(BF16)
    keep[kind + (2,)] = wide[:, 128:].astype(BF16)
    keep[kind + (3,)] = ahead[:, :128].astype(BF16)


def block_of(small, tile, half, block, base, first, count):
    lanes = 2 * tile + half
    pixel = 2 * (lanes // 3)
    place = lane_block(tile, block)

    def take(pix, arrangement):
        row = place - 3 * (pix + first)
        if 0 <= row < count:
            return small(arrangement, base + 16 * row)
        return None

    if lanes % 3 == 0:
        parts = [take(pixel, 0)]
    elif lanes % 3 == 2:
        parts = [take(pixel + 1, 1)]
    else:
        parts = [take(pixel, 2), take(pixel + 1, 3)]
    parts = [part for part in parts if part is not None]
    if not parts:
        return jnp.zeros((16, 128), BF16)
    return parts[0] if len(parts) == 1 else parts[0] + parts[1]


def kernel(
    lengths_hbm, patches, stem_hbm, spatial_hbm, temporal_hbm, out,
    lengths, own, halo, stem, spatial, temporal, folded, small, small_stem, wide, wide_stem, rows, acc, feats,
    load_sem, send_sem, recv_sem,
):
    clip, row = lax.axis_index("clip"), lax.axis_index("row")
    me = clip * 8 + row

    def place(device):
        return (device // 8, lax.rem(device, 8))

    loads = [
        pltpu.make_async_copy(spatial_hbm, spatial, load_sem.at[0]),
        pltpu.make_async_copy(stem_hbm, stem, load_sem.at[1]),
        pltpu.make_async_copy(temporal_hbm, temporal, load_sem.at[2]),
        pltpu.make_async_copy(patches, own.at[:, :, pl.ds(128, LANES)], load_sem.at[3]),
        pltpu.make_async_copy(lengths_hbm, lengths, load_sem.at[4]),
    ]
    barrier = pltpu.get_barrier_semaphore()

    @pl.when(me > 0)
    def _():
        pl.semaphore_signal(barrier, inc=1, device_id=place(me - 1), device_id_type=MESH)

    cuts = CUTS
    edges = [0] + [384 * cut + 128 for cut in cuts[1:-1]] + [LANES]
    sends = [
        pltpu.make_async_remote_copy(
            patches.at[:, :, pl.ds(lo, hi - lo)],
            halo.at[:, :, pl.ds(128 + lo, hi - lo)],
            send_sem.at[c],
            recv_sem.at[c],
            device_id=place(jnp.minimum(me + 1, LAST)),
            device_id_type=MESH,
        )
        for c, (lo, hi) in enumerate(zip(edges[:-1], edges[1:]))
    ]

    def start_sends():
        pl.semaphore_wait(barrier, 1)
        for send in sends:
            send.start()

    ends = row >= 6
    pl.when(jnp.logical_and(ends, me < LAST))(start_sends)
    for load in loads:
        load.start()

    loads[4].wait()
    first, total = jnp.int32(0), jnp.int32(0)
    first_next = jnp.int32(0)
    for k in range(16):
        first = jnp.where(total <= 2 * me, total, first)
        first_next = jnp.where(total <= 2 * me + 1, total, first_next)
        total = total + lengths[k]
    room0 = 2 * me - first
    room1 = 2 * me + 1 - first_next

    side = jnp.zeros((2, SLAB, 128), BF16)
    for ref in (own, halo):
        ref[:, :, :128] = side
        ref[:, :, LANES + 128:] = side

    loads[0].wait()
    loads[1].wait()
    for tap in range(9):
        folded[48 * tap : 48 * tap + 48] = mix(stem[...], spatial[tap // 3, tap % 3])
    spread(stem[...].astype(F32), small_stem, ())
    pl.when(jnp.logical_not(ends))(start_sends)
    loads[2].wait()
    upper = folded[...].astype(BF16)
    lower = (folded[...] - upper.astype(F32)).astype(BF16)
    for t in range(3):
        spread(mix(upper, temporal[t]) + mix(lower, temporal[t]), small, (t,))

    def widen(tap, carry):
        t, a = tap // 3, lax.rem(tap, 3)
        base = a * 144
        for tile in range(TILES):
            for half in range(2):
                for block in range(16):
                    value = block_of(
                        lambda arrangement, row: small[t, arrangement, pl.ds(pl.multiple_of(row, 16), 16)],
                        tile, half, block, base, -1, 9,
                    )
                    where = pl.ds(pl.multiple_of(tap * 256 + 16 * block, 16), 16)
                    wide[tile, where, 128 * half : 128 * half + 128] = value
        return carry

    lax.fori_loop(0, 9, widen, 0)
    for tile in range(TILES):
        for half in range(2):
            for block in range(16):
                wide_stem[tile, 16 * block : 16 * block + 16, 128 * half : 128 * half + 128] = block_of(
                    lambda arrangement, row: small_stem[arrangement, row : row + 16], tile, half, block, 0, 0, 3
                )

    band = lax.broadcasted_iota(jnp.int32, (SLAB, 128), 0)
    left = lax.broadcasted_iota(jnp.int32, (SLAB, 128), 1) < 64

    def put(source, t, frame, group):
        tiles = [source[:, 128 * i : 128 * i + 128] for i in range(5)]
        turned = [pltpu.roll(tiles[i], 64, 1) for i in (2, 3, 4)]
        even = (tiles[1], tiles[2], jnp.where(left, tiles[2], tiles[0]))
        odd = (
            jnp.where(left, turned[0], turned[1]),
            jnp.where(left, turned[1], turned[2]),
            jnp.where(left, turned[1], turned[0]),
        )
        where = pl.ds(pl.multiple_of(frame * HALF + group * 16, 16), 16)
        for k in range(3):
            down = [jnp.where(band == 0, 0.0, pltpu.roll(x[k], 1, 0)) for x in (even, odd)]
            up = [jnp.where(band == SLAB - 1, 0.0, pltpu.roll(x[k], SLAB - 1, 0)) for x in (even, odd)]
            for a, both in enumerate((down, [even[k], odd[k]], up)):
                rows[t, a, k, where] = jnp.concatenate(both, axis=0).astype(BF16)

    def lanes_of(ref, frame, group):
        return ref[frame, :, pl.ds(pl.multiple_of(group * 384, 128), 640)].astype(F32)

    loads[3].wait()

    def own_rows(group, carry):
        own0, own1 = lanes_of(own, 0, group), lanes_of(own, 1, group)
        put(own0, 0, 0, group)
        put(own1, 0, 1, group)
        put(jnp.where(room1 >= 1, own0, own1), 1, 1, group)
        return carry

    lax.fori_loop(0, GROUPS, own_rows, 0, unroll=10)

    def left_side(t, tile, lo, count):
        return jnp.concatenate(
            [rows[t, a, k, lo : lo + count] for a in range(3) for k in READS[tile]], axis=1
        )

    for tile in range(TILES):
        centre = jnp.concatenate([rows[0, 1, k] for k in READS[tile]], axis=1)
        feats[tile] = mix(centre, wide_stem[tile]).astype(BF16)
        for at in range(0, HALF, STEP):
            acc[tile, at : at + STEP] = mix(left_side(0, tile, at, STEP), wide[tile, 0:768])
        for at in range(HALF, 2 * HALF, STEP):
            both = jnp.concatenate([left_side(0, tile, at, STEP), left_side(1, tile, at, STEP)], axis=1)
            acc[tile, at : at + STEP] = mix(both, wide[tile, 0:1536])

    def halo_rows(group, carry):
        own0, own1 = lanes_of(own, 0, group), lanes_of(own, 1, group)
        halo0, halo1 = lanes_of(halo, 0, group), lanes_of(halo, 1, group)
        tap01 = jnp.where(room0 >= 1, halo1, own0)
        put(tap01, 1, 0, group)
        put(jnp.where(room0 >= 2, halo0, tap01), 2, 0, group)
        tap11 = jnp.where(room1 >= 1, own0, own1)
        put(jnp.where(room1 >= 2, halo1, tap11), 2, 1, group)
        return carry

    for c in range(CHUNKS):
        @pl.when(me > 0)
        def _():
            sends[c].wait_recv()

        lax.fori_loop(cuts[c], cuts[c + 1], halo_rows, 0, unroll=10)
        lo, count = 16 * cuts[c], 16 * (cuts[c + 1] - cuts[c])
        for tile in range(TILES):
            tap1 = mix(left_side(1, tile, lo, count), wide[tile, 768:1536])
            sides = [left_side(2, tile, lo + at, count) for at in (0, HALF)]
            tap2 = mix(jnp.concatenate(sides, axis=0), wide[tile, 1536:])
            for frame in range(2):
                at = frame * HALF + lo
                value = acc[tile, at : at + count] + tap2[frame * count : (frame + 1) * count]
                if frame == 0:
                    value = value + tap1
                branch = (value * (0.5 * jnp.tanh(0.5 * value) + 0.5)).astype(BF16)
                result = (feats[tile, at : at + count].astype(F32) + branch.astype(F32)).astype(BF16)
                for g in range(count // 8):
                    to = (lo // 8 + g) * 768 + 256 * tile
                    out[frame, :, to : to + 256] = result[8 * g : 8 * g + 8]

    @pl.when(me < LAST)
    def _():
        for send in sends:
            send.wait_send()


def body(patches, clip_lengths, stem_weight, spatial_weight, temporal_weight):
    operands = (clip_lengths, patches, stem_weight, spatial_weight, temporal_weight)
    return pl.pallas_call(
        kernel,
        out_shape=pltpu.VMEM((2, SLAB, COLS * CH), BF16),
        in_specs=[pl.BlockSpec(memory_space=pltpu.HBM)] * 5,
        scratch_shapes=[
            pltpu.SMEM((16,), jnp.int32),
            pltpu.VMEM((2, SLAB, LANES + 256), BF16),
            pltpu.VMEM((2, SLAB, LANES + 256), BF16),
            pltpu.VMEM((PATCH, CH), BF16),
            pltpu.VMEM((3, 3, CH, CH), BF16),
            pltpu.VMEM((3, CH, CH), BF16),
            pltpu.VMEM((9 * PATCH, CH), F32),
            pltpu.VMEM((3, 4, 9 * PATCH, 128), BF16),
            pltpu.VMEM((4, PATCH, 128), BF16),
            pltpu.VMEM((TILES, 9 * 256, 256), BF16),
            pltpu.VMEM((TILES, 256, 256), BF16),
            pltpu.VMEM((3, 3, 3, 2 * HALF, 128), BF16),
            pltpu.VMEM((TILES, 2 * HALF, 256), F32),
            pltpu.VMEM((TILES, 2 * HALF, 256), BF16),
            pltpu.SemaphoreType.DMA((5,)),
            pltpu.SemaphoreType.DMA((CHUNKS,)),
            pltpu.SemaphoreType.DMA((CHUNKS,)),
        ],
        compiler_params=pltpu.CompilerParams(
            collective_id=0, has_side_effects=True, vmem_limit_bytes=44 << 20
        ),
        cost_estimate=pl.CostEstimate(flops=10_000_000_000, bytes_accessed=4_000_000, transcendentals=1_000_000),
    )(*[pltpu.with_memory_space_constraint(x, pltpu.HBM) for x in operands])


def solution(mesh):
    return jax.shard_map(
        body,
        mesh=mesh,
        in_specs=(P(("clip", "row"), None, None), P(), P(), P(), P()),
        out_specs=P(("clip", "row"), None, None),
        check_vma=False,
    )
```

time: 21.4 us -> 15.3 us (0.71)
  local copies, waits for them, and re-layouts: 5.82 us -> 1.27 us
  Pallas kernels: 15.3 us -> 13.9 us
    unnamed x11 -> x1, local copies, waits for them, and re-layouts: 5.82 us -> 1.27 us
    pallas_call x1, Pallas kernels: 15.3 us -> 13.9 us  [body(): pl.pallas_call(kernel, out_shape=pltpu.VMEM((2, SLAB, COLS * CH), BF16),...]
where the time goes in v2:
time: 15.3 us; the launch traced here: 15.1 us
  Pallas kernels  13.9 us (91%)
  local copies, waits for them, and re-layouts  1.27 us (8%)
    pallas_call x1, Pallas kernels, body(): pl.pallas_call(kernel, out_shape=pltpu.VMEM((2, SLAB, COLS * CH), BF16),...  13.9 us
    unnamed x1, local copies, waits for them, and re-layouts  1.27 us

profile of v2, /device:TPU:24, one launch (start us, length us, event | category | flops | bytes accessed | tf_op | source)
XLA Modules:
  0.0 15.1 jit_solution(12115999884971463714)
XLA Ops:
  0.0 13.9 %shard_map.55 = bf16[2,8,61440]{2,1,0:T(8,128)(2,1)S(1)} custom-call(s32[16]{0:T(128)} %lengths_hbm.1, bf16[2,8,15360]{2,1,0:T(8,128)(2,1)} %patches.1, bf16[48,192]{1,0:T(8,128)(2,1)} %stem_hbm.1, bf16[3,3,192,192]{3,2,1,0:T(8,128)(2,1)} %spatial_hbm.1, bf16[3,192,192]{2,1,0:T(8,128)(2,1)} %temporal_hbm.1), custom_call_target="tpu_custom_call" | custom-call | flops 10000000000 | bytes 4000000 | tf_op jit(solution)/shard_map/pallas_call | solution.py:252
  13.9 1.3 %copy.7 = bf16[2,8,61440]{2,1,0:T(8,128)(2,1)} copy(bf16[2,8,61440]{2,1,0:T(8,128)(2,1)S(1)} %shard_map.55) | data formatting | bytes 3932160

commit v3 on v2

--- a/solution.py
+++ b/solution.py
@@ -1,3 +1,5 @@
+import functools
+
 import jax
 import jax.numpy as jnp
 from jax import lax
@@ -16,11 +18,12 @@
 GROUPS = 40
 TILES = 3
 HALF = 640
-CUTS = (0, 10, 20, 30, 40)
-CHUNKS = len(CUTS) - 1
+CUTS1 = (0, 14, 28, 40)
+CUTS0 = (0, 14, 28, 40)
+CHUNKS = len(CUTS1) + len(CUTS0) - 2
 LAST = 127
 STEP = 160
-READS = ((0, 2), (0, 1), (0, 1))
+SPANS = ((0, 256, (0, 2)), (256, 768, (0, 1)))
 
 
 def lane_block(tile, block):
@@ -61,7 +64,7 @@
         parts = [take(pixel, 2), take(pixel + 1, 3)]
     parts = [part for part in parts if part is not None]
     if not parts:
-        return jnp.zeros((16, 128), BF16)
+        return None
     return parts[0] if len(parts) == 1 else parts[0] + parts[1]
 
 
@@ -89,19 +92,22 @@
     def _():
         pl.semaphore_signal(barrier, inc=1, device_id=place(me - 1), device_id_type=MESH)
 
-    cuts = CUTS
-    edges = [0] + [384 * cut + 128 for cut in cuts[1:-1]] + [LANES]
-    sends = [
-        pltpu.make_async_remote_copy(
-            patches.at[:, :, pl.ds(lo, hi - lo)],
-            halo.at[:, :, pl.ds(128 + lo, hi - lo)],
-            send_sem.at[c],
-            recv_sem.at[c],
-            device_id=place(jnp.minimum(me + 1, LAST)),
-            device_id_type=MESH,
-        )
-        for c, (lo, hi) in enumerate(zip(edges[:-1], edges[1:]))
-    ]
+    sends, pieces = [], []
+    for frame, cuts in ((1, CUTS1), (0, CUTS0)):
+        edges = [0] + [384 * cut + 128 for cut in cuts[1:-1]] + [LANES]
+        for c in range(len(cuts) - 1):
+            lo, hi = edges[c], edges[c + 1]
+            pieces.append((frame, cuts[c], cuts[c + 1]))
+            sends.append(
+                pltpu.make_async_remote_copy(
+                    patches.at[frame, :, pl.ds(lo, hi - lo)],
+                    halo.at[frame, :, pl.ds(128 + lo, hi - lo)],
+                    send_sem.at[len(sends)],
+                    recv_sem.at[len(sends)],
+                    device_id=place(jnp.minimum(me + 1, LAST)),
+                    device_id_type=MESH,
+                )
+            )
 
     def start_sends():
         pl.semaphore_wait(barrier, 1)
@@ -128,12 +134,22 @@
         ref[:, :, :128] = side
         ref[:, :, LANES + 128:] = side
 
+    def clear(tap, carry):
+        for tile in range(TILES):
+            for half in range(2):
+                for block in range(16):
+                    if block_of(lambda arrangement, row: 0, tile, half, block, 0, -1, 9) is None:
+                        to = pl.ds(pl.multiple_of(tap * 256 + 16 * block, 16), 16)
+                        lanes = 256 * tile + 128 * half
+                        wide[to, lanes : lanes + 128] = jnp.zeros((16, 128), BF16)
+        return carry
+
+    lax.fori_loop(0, 9, clear, 0)
     loads[0].wait()
     loads[1].wait()
     for tap in range(9):
         folded[48 * tap : 48 * tap + 48] = mix(stem[...], spatial[tap // 3, tap % 3])
     spread(stem[...].astype(F32), small_stem, ())
-    pl.when(jnp.logical_not(ends))(start_sends)
     loads[2].wait()
     upper = folded[...].astype(BF16)
     lower = (folded[...] - upper.astype(F32)).astype(BF16)
@@ -150,22 +166,30 @@
                         lambda arrangement, row: small[t, arrangement, pl.ds(pl.multiple_of(row, 16), 16)],
                         tile, half, block, base, -1, 9,
                     )
-                    where = pl.ds(pl.multiple_of(tap * 256 + 16 * block, 16), 16)
-                    wide[tile, where, 128 * half : 128 * half + 128] = value
+                    to = pl.ds(pl.multiple_of(tap * 256 + 16 * block, 16), 16)
+                    lanes = 256 * tile + 128 * half
+                    if value is not None:
+                        wide[to, lanes : lanes + 128] = value
         return carry
 
     lax.fori_loop(0, 9, widen, 0)
     for tile in range(TILES):
         for half in range(2):
             for block in range(16):
-                wide_stem[tile, 16 * block : 16 * block + 16, 128 * half : 128 * half + 128] = block_of(
+                value = block_of(
                     lambda arrangement, row: small_stem[arrangement, row : row + 16], tile, half, block, 0, 0, 3
                 )
+                lanes = 256 * tile + 128 * half
+                wide_stem[16 * block : 16 * block + 16, lanes : lanes + 128] = (
+                    jnp.zeros((16, 128), BF16) if value is None else value
+                )
+
+    pl.when(jnp.logical_not(ends))(start_sends)
 
     band = lax.broadcasted_iota(jnp.int32, (SLAB, 128), 0)
     left = lax.broadcasted_iota(jnp.int32, (SLAB, 128), 1) < 64
 
-    def put(source, t, frame, group):
+    def arranged(source):
         tiles = [source[:, 128 * i : 128 * i + 128] for i in range(5)]
         turned = [pltpu.roll(tiles[i], 64, 1) for i in (2, 3, 4)]
         even = (tiles[1], tiles[2], jnp.where(left, tiles[2], tiles[0]))
@@ -174,12 +198,16 @@
             jnp.where(left, turned[1], turned[2]),
             jnp.where(left, turned[1], turned[0]),
         )
-        where = pl.ds(pl.multiple_of(frame * HALF + group * 16, 16), 16)
+        blocks = {}
         for k in range(3):
             down = [jnp.where(band == 0, 0.0, pltpu.roll(x[k], 1, 0)) for x in (even, odd)]
             up = [jnp.where(band == SLAB - 1, 0.0, pltpu.roll(x[k], SLAB - 1, 0)) for x in (even, odd)]
             for a, both in enumerate((down, [even[k], odd[k]], up)):
-                rows[t, a, k, where] = jnp.concatenate(both, axis=0).astype(BF16)
+                blocks[a, k] = jnp.concatenate(both, axis=0).astype(BF16)
+        return blocks
+
+    def where(frame, group):
+        return pl.ds(pl.multiple_of(frame * HALF + group * 16, 16), 16)
 
     def lanes_of(ref, frame, group):
         return ref[frame, :, pl.ds(pl.multiple_of(group * 384, 128), 640)].astype(F32)
@@ -187,59 +215,64 @@
     loads[3].wait()
 
     def own_rows(group, carry):
-        own0, own1 = lanes_of(own, 0, group), lanes_of(own, 1, group)
-        put(own0, 0, 0, group)
-        put(own1, 0, 1, group)
-        put(jnp.where(room1 >= 1, own0, own1), 1, 1, group)
+        own0, own1 = arranged(lanes_of(own, 0, group)), arranged(lanes_of(own, 1, group))
+        for a, k in own0:
+            rows[0, a, k, where(0, group)] = own0[a, k]
+            rows[0, a, k, where(1, group)] = own1[a, k]
+            rows[1, a, k, where(1, group)] = jnp.where(room1 >= 1, own0[a, k], own1[a, k])
         return carry
 
     lax.fori_loop(0, GROUPS, own_rows, 0, unroll=10)
 
-    def left_side(t, tile, lo, count):
-        return jnp.concatenate(
-            [rows[t, a, k, lo : lo + count] for a in range(3) for k in READS[tile]], axis=1
-        )
-
-    for tile in range(TILES):
-        centre = jnp.concatenate([rows[0, 1, k] for k in READS[tile]], axis=1)
-        feats[tile] = mix(centre, wide_stem[tile]).astype(BF16)
+    def left_side(t, reads, lo, count):
+        return jnp.concatenate([rows[t, a, k, lo : lo + count] for a in range(3) for k in reads], axis=1)
+
+    for start, end, reads in SPANS:
+        for at in range(0, 2 * HALF, STEP):
+            centre = jnp.concatenate([rows[0, 1, k, at : at + STEP] for k in reads], axis=1)
+            feats[at : at + STEP, start:end] = mix(centre, wide_stem[:, start:end]).astype(BF16)
         for at in range(0, HALF, STEP):
-            acc[tile, at : at + STEP] = mix(left_side(0, tile, at, STEP), wide[tile, 0:768])
+            acc[at : at + STEP, start:end] = mix(left_side(0, reads, at, STEP), wide[0:768, start:end])
         for at in range(HALF, 2 * HALF, STEP):
-            both = jnp.concatenate([left_side(0, tile, at, STEP), left_side(1, tile, at, STEP)], axis=1)
-            acc[tile, at : at + STEP] = mix(both, wide[tile, 0:1536])
-
-    def halo_rows(group, carry):
-        own0, own1 = lanes_of(own, 0, group), lanes_of(own, 1, group)
-        halo0, halo1 = lanes_of(halo, 0, group), lanes_of(halo, 1, group)
-        tap01 = jnp.where(room0 >= 1, halo1, own0)
-        put(tap01, 1, 0, group)
-        put(jnp.where(room0 >= 2, halo0, tap01), 2, 0, group)
-        tap11 = jnp.where(room1 >= 1, own0, own1)
-        put(jnp.where(room1 >= 2, halo1, tap11), 2, 1, group)
+            both = jnp.concatenate([left_side(0, reads, at, STEP), left_side(1, reads, at, STEP)], axis=1)
+            acc[at : at + STEP, start:end] = mix(both, wide[0:1536, start:end])
+
+    def halo_rows(halo_frame, group, carry):
+        new = arranged(lanes_of(halo, halo_frame, group))
+        for a, k in new:
+            if halo_frame == 1:
+                rows[1, a, k, where(0, group)] = jnp.where(room0 >= 1, new[a, k], rows[0, a, k, where(0, group)])
+                rows[2, a, k, where(1, group)] = jnp.where(room1 >= 2, new[a, k], rows[1, a, k, where(1, group)])
+            else:
+                rows[2, a, k, where(0, group)] = jnp.where(room0 >= 2, new[a, k], rows[1, a, k, where(0, group)])
         return carry
 
-    for c in range(CHUNKS):
+    def finish(frame, lo, count):
+        at = frame * HALF + lo
+        for start, end, reads in SPANS:
+            value = acc[at : at + count, start:end] + mix(left_side(2, reads, at, count), wide[1536:, start:end])
+            branch = (value * (0.5 * jnp.tanh(0.5 * value) + 0.5)).astype(BF16)
+            result = (feats[at : at + count, start:end].astype(F32) + branch.astype(F32)).astype(BF16)
+            for g in range(count // 8):
+                to = (lo // 8 + g) * 768
+                out[frame, :, to + start : to + end] = result[8 * g : 8 * g + 8]
+
+    for send, (halo_frame, first_group, end_group) in zip(sends, pieces):
         @pl.when(me > 0)
         def _():
-            sends[c].wait_recv()
-
-        lax.fori_loop(cuts[c], cuts[c + 1], halo_rows, 0, unroll=10)
-        lo, count = 16 * cuts[c], 16 * (cuts[c + 1] - cuts[c])
-        for tile in range(TILES):
-            tap1 = mix(left_side(1, tile, lo, count), wide[tile, 768:1536])
-            sides = [left_side(2, tile, lo + at, count) for at in (0, HALF)]
-            tap2 = mix(jnp.concatenate(sides, axis=0), wide[tile, 1536:])
-            for frame in range(2):
-                at = frame * HALF + lo
-                value = acc[tile, at : at + count] + tap2[frame * count : (frame + 1) * count]
-                if frame == 0:
-                    value = value + tap1
-                branch = (value * (0.5 * jnp.tanh(0.5 * value) + 0.5)).astype(BF16)
-                result = (feats[tile, at : at + count].astype(F32) + branch.astype(F32)).astype(BF16)
-                for g in range(count // 8):
-                    to = (lo // 8 + g) * 768 + 256 * tile
-                    out[frame, :, to : to + 256] = result[8 * g : 8 * g + 8]
+            send.wait_recv()
+
+        number = end_group - first_group
+        lax.fori_loop(
+            first_group, end_group, functools.partial(halo_rows, halo_frame), 0, unroll=number if number <= 14 else 10
+        )
+        lo, count = 16 * first_group, 16 * number
+        if halo_frame == 1:
+            for start, end, reads in SPANS:
+                acc[lo : lo + count, start:end] += mix(left_side(1, reads, lo, count), wide[768:1536, start:end])
+            finish(1, lo, count)
+        else:
+            finish(0, lo, count)
 
     @pl.when(me < LAST)
     def _():
@@ -263,11 +296,11 @@
             pltpu.VMEM((9 * PATCH, CH), F32),
             pltpu.VMEM((3, 4, 9 * PATCH, 128), BF16),
             pltpu.VMEM((4, PATCH, 128), BF16),
-            pltpu.VMEM((TILES, 9 * 256, 256), BF16),
-            pltpu.VMEM((TILES, 256, 256), BF16),
+            pltpu.VMEM((9 * 256, 256 * TILES), BF16),
+            pltpu.VMEM((256, 256 * TILES), BF16),
             pltpu.VMEM((3, 3, 3, 2 * HALF, 128), BF16),
-            pltpu.VMEM((TILES, 2 * HALF, 256), F32),
-            pltpu.VMEM((TILES, 2 * HALF, 256), BF16),
+            pltpu.VMEM((2 * HALF, 256 * TILES), F32),
+            pltpu.VMEM((2 * HALF, 256 * TILES), BF16),
             pltpu.SemaphoreType.DMA((5,)),
             pltpu.SemaphoreType.DMA((CHUNKS,)),
             pltpu.SemaphoreType.DMA((CHUNKS,)),

time: 15.3 us -> 14.8 us (0.967)
  Pallas kernels: 13.9 us -> 13.4 us
    pallas_call x1, Pallas kernels: 13.9 us -> 13.4 us  [body(): pl.pallas_call(kernel, out_shape=pltpu.VMEM((2, SLAB, COLS * CH), BF16),...]
where the time goes in v3:
time: 14.8 us; the launch traced here: 14.7 us
  Pallas kernels  13.4 us (91%)
  local copies, waits for them, and re-layouts  1.27 us (9%)
    pallas_call x1, Pallas kernels, body(): pl.pallas_call(kernel, out_shape=pltpu.VMEM((2, SLAB, COLS * CH), BF16),...  13.4 us
    unnamed x1, local copies, waits for them, and re-layouts  1.27 us

profile of v3, /device:TPU:24, one launch (start us, length us, event | category | flops | bytes accessed | tf_op | source)
XLA Modules:
  0.0 14.7 jit_solution(10483393677000475630)
XLA Ops:
  0.0 13.4 %shard_map.55 = bf16[2,8,61440]{2,1,0:T(8,128)(2,1)S(1)} custom-call(s32[16]{0:T(128)} %lengths_hbm.1, bf16[2,8,15360]{2,1,0:T(8,128)(2,1)} %patches.1, bf16[48,192]{1,0:T(8,128)(2,1)} %stem_hbm.1, bf16[3,3,192,192]{3,2,1,0:T(8,128)(2,1)} %spatial_hbm.1, bf16[3,192,192]{2,1,0:T(8,128)(2,1)} %temporal_hbm.1), custom_call_target="tpu_custom_call" | custom-call | flops 10000000000 | bytes 4000000 | tf_op jit(solution)/shard_map/pallas_call | solution.py:285
  13.4 1.3 %copy.7 = bf16[2,8,61440]{2,1,0:T(8,128)(2,1)} copy(bf16[2,8,61440]{2,1,0:T(8,128)(2,1)S(1)} %shard_map.55) | data formatting | bytes 3932160

commit v4 on v3

--- a/solution.py
+++ b/solution.py
@@ -18,10 +18,12 @@
 GROUPS = 40
 TILES = 3
 HALF = 640
-CUTS1 = (0, 14, 28, 40)
+CUTS1 = (0, 20, 40)
 CUTS0 = (0, 14, 28, 40)
+DIRECT = 1
 CHUNKS = len(CUTS1) + len(CUTS0) - 2
 LAST = 127
+MOST = 14
 STEP = 160
 SPANS = ((0, 256, (0, 2)), (256, 768, (0, 1)))
 
@@ -98,9 +100,10 @@
         for c in range(len(cuts) - 1):
             lo, hi = edges[c], edges[c + 1]
             pieces.append((frame, cuts[c], cuts[c + 1]))
+            source, begin = (patches, 0) if len(sends) < DIRECT else (own, 128)
             sends.append(
                 pltpu.make_async_remote_copy(
-                    patches.at[frame, :, pl.ds(lo, hi - lo)],
+                    source.at[frame, :, pl.ds(begin + lo, hi - lo)],
                     halo.at[frame, :, pl.ds(128 + lo, hi - lo)],
                     send_sem.at[len(sends)],
                     recv_sem.at[len(sends)],
@@ -111,14 +114,20 @@
 
     def start_sends():
         pl.semaphore_wait(barrier, 1)
-        for send in sends:
+        for send in sends[:DIRECT]:
+            send.start()
+
+    def start_others():
+        loads[3].wait()
+        for send in sends[DIRECT:]:
             send.start()
 
     ends = row >= 6
     pl.when(jnp.logical_and(ends, me < LAST))(start_sends)
-    for load in loads:
+    for load in loads[::-1]:
         load.start()
 
+    pl.when(jnp.logical_and(ends, me < LAST))(start_others)
     loads[4].wait()
     first, total = jnp.int32(0), jnp.int32(0)
     first_next = jnp.int32(0)
@@ -184,7 +193,10 @@
                     jnp.zeros((16, 128), BF16) if value is None else value
                 )
 
-    pl.when(jnp.logical_not(ends))(start_sends)
+    @pl.when(jnp.logical_not(ends))
+    def _():
+        start_sends()
+        start_others()
 
     band = lax.broadcasted_iota(jnp.int32, (SLAB, 128), 0)
     left = lax.broadcasted_iota(jnp.int32, (SLAB, 128), 1) < 64
@@ -212,7 +224,7 @@
     def lanes_of(ref, frame, group):
         return ref[frame, :, pl.ds(pl.multiple_of(group * 384, 128), 640)].astype(F32)
 
-    loads[3].wait()
+    pl.when(me == LAST)(loads[3].wait)
 
     def own_rows(group, carry):
         own0, own1 = arranged(lanes_of(own, 0, group)), arranged(lanes_of(own, 1, group))
@@ -262,17 +274,15 @@
         def _():
             send.wait_recv()
 
-        number = end_group - first_group
-        lax.fori_loop(
-            first_group, end_group, functools.partial(halo_rows, halo_frame), 0, unroll=number if number <= 14 else 10
-        )
-        lo, count = 16 * first_group, 16 * number
-        if halo_frame == 1:
-            for start, end, reads in SPANS:
-                acc[lo : lo + count, start:end] += mix(left_side(1, reads, lo, count), wide[768:1536, start:end])
-            finish(1, lo, count)
-        else:
-            finish(0, lo, count)
+        parts = -((first_group - end_group) // MOST)
+        marks = [first_group + (end_group - first_group) * i // parts for i in range(parts + 1)]
+        for low, high in zip(marks[:-1], marks[1:]):
+            lax.fori_loop(low, high, functools.partial(halo_rows, halo_frame), 0, unroll=high - low)
+            lo, count = 16 * low, 16 * (high - low)
+            if halo_frame == 1:
+                for start, end, reads in SPANS:
+                    acc[lo : lo + count, start:end] += mix(left_side(1, reads, lo, count), wide[768:1536, start:end])
+            finish(halo_frame, lo, count)
 
     @pl.when(me < LAST)
     def _():

time: 14.8 us -> 14.8 us (level)
  no operation moved by 1% of the time
where the time goes in v4:
time: 14.8 us; the launch traced here: 14.7 us
  Pallas kernels  13.4 us (91%)
  local copies, waits for them, and re-layouts  1.27 us (9%)
    pallas_call x1, Pallas kernels, body(): pl.pallas_call(kernel, out_shape=pltpu.VMEM((2, SLAB, COLS * CH), BF16),...  13.4 us
    unnamed x1, local copies, waits for them, and re-layouts  1.27 us

profile of v4, /device:TPU:24, one launch (start us, length us, event | category | flops | bytes accessed | tf_op | source)
XLA Modules:
  0.0 14.7 jit_solution(10713945255097196489)
XLA Ops:
  0.0 13.4 %shard_map.55 = bf16[2,8,61440]{2,1,0:T(8,128)(2,1)S(1)} custom-call(s32[16]{0:T(128)} %lengths_hbm.1, bf16[2,8,15360]{2,1,0:T(8,128)(2,1)} %patches.1, bf16[48,192]{1,0:T(8,128)(2,1)} %stem_hbm.1, bf16[3,3,192,192]{3,2,1,0:T(8,128)(2,1)} %spatial_hbm.1, bf16[3,192,192]{2,1,0:T(8,128)(2,1)} %temporal_hbm.1), custom_call_target="tpu_custom_call" | custom-call | flops 10000000000 | bytes 4000000 | tf_op jit(solution)/shard_map/pallas_call | solution.py:295
  13.4 1.3 %copy.7 = bf16[2,8,61440]{2,1,0:T(8,128)(2,1)} copy(bf16[2,8,61440]{2,1,0:T(8,128)(2,1)S(1)} %shard_map.55) | data formatting | bytes 3932160
